TPU v7x, 512 devices: a whole 4x4x16 slice. The times are simulated.
512 devices in a mesh: dp: 2 (over core), resp: 32 (over z, x_hi), tensor: 8 (over y, x_lo).
Axes of the slice: x: 4 (x_hi: 2, x_lo: 2; x = x_hi * 2 + x_lo), y: 4, z: 16, core: 2. Of those that a mesh axis runs over, the one named last changes fastest.
Arguments:
- queries: bfloat16 [32768, 5120], P(('dp', 'resp'), 'tensor'), parts along dimension 0, may hold values from -8 to 8
- response_kv: bfloat16 [32768, 2048], P(('dp', 'resp', 'tensor')), parts along dimension 0, may hold values from -6 to 6
- prompt_kv: bfloat16 [4096, 2048], P(('dp', 'resp', 'tensor')), parts along dimension 0, may hold values from -4 to 4
- group_ids: int32 [256], P('dp'), parts along dimension 0, may hold values from 0 to 7, as said below
- lengths: int32 [256], P('dp'), parts along dimension 0, may hold values from 32 to 128
- tree_parent: int32 [256, 4], P('dp'), parts along dimension 0, may hold values from 0 to 2, as said below
Outputs:
- attended: bfloat16 [32768, 5120], P(('dp', 'resp'), 'tensor'), parts along dimension 0
There are 2 independent parts, one for each index of `dp`. A program takes and returns all parts, laid end to end along the dimension named above; each array names one. Nothing has to cross between parts.
Inputs may be any that keep to these rules, and one draw needn't show every extreme that they name: `group_ids`: each prompt number is the prompt of exactly 16 responses. tree_parent[r, 0] = 0 and tree_parent[r, b] < b for b >= 1.
All inputs are finite; a program needn't handle non-finite values.
Results may differ from a plain program's by a relative error of at most 0.0055.
Values may be sent and summed in bfloat16 or wider, within the bound.
A program may use at most 64 MiB of HBM per device.

v0:
```python
import math

import jax
import jax.numpy as jnp
from jax import lax
from jax.sharding import PartitionSpec as P

H = 40
KVH = 8
HD = 128
RLEN = 128
NB = 4
PLEN = 256
RESP_DEV = 4


neg_big = -1e30


def tree_sight(parents, blocks):
    ids = jnp.arange(blocks, dtype=jnp.int32)
    step = (parents[:, :, None] == ids[None, None, :]) & (ids[None, :, None] > 0)
    sight = step
    for turn in range(blocks):
        sight = sight | jnp.any(sight[:, :, :, None] & step[:, None, :, :], axis=2)
    return sight


def absorb(state, scores, mask, values, form):
    top, total, acc = state
    masked = jnp.where(mask, scores, neg_big)
    new_top = jnp.maximum(top, jnp.max(masked, axis=-1))
    weights = jnp.where(mask, jnp.exp(scores - new_top[..., None]), 0.0)
    factor = jnp.exp(top - new_top)
    total = total * factor + jnp.sum(weights, axis=-1)
    rounded = weights.astype(jnp.bfloat16)
    acc = acc * factor[..., None] + jnp.einsum(
        form, rounded, values, preferred_element_type=jnp.float32
    )
    return (new_top, total, acc)


def local(queries, response_kv, prompt_kv, group_ids, lengths, tree_parent):
    tensor_count = lax.axis_size("tensor")
    kv_dev = KVH // tensor_count
    group = H // KVH
    width = RLEN // NB
    scale = 1.0 / math.sqrt(HD)
    first = lax.axis_index("resp") * RESP_DEV
    my_groups = lax.dynamic_slice_in_dim(group_ids, first, RESP_DEV, 0)
    my_lengths = lax.dynamic_slice_in_dim(lengths, first, RESP_DEV, 0)
    my_parents = lax.dynamic_slice_in_dim(tree_parent, first, RESP_DEV, 0)
    heads_q = queries.reshape(RESP_DEV, RLEN, kv_dev, group, HD)
    own_rows = lax.all_to_all(response_kv, "tensor", split_axis=1, concat_axis=0, tiled=True)
    own_rows = own_rows.reshape(RESP_DEV, RLEN, kv_dev, 2, HD)
    slots = jnp.arange(RLEN, dtype=jnp.int32)
    block_of = slots // width
    sight = tree_sight(my_parents, NB)
    same = (block_of[:, None] == block_of[None, :]) & (slots[None, :] <= slots[:, None])
    seen = sight[:, block_of[:, None], block_of[None, :]]
    own_mask = (same[None] | seen) & (slots[None, None, :] < my_lengths[:, None, None])
    state = (
        jnp.full((RESP_DEV, kv_dev, group, RLEN), neg_big, jnp.float32),
        jnp.zeros((RESP_DEV, kv_dev, group, RLEN), jnp.float32),
        jnp.zeros((RESP_DEV, kv_dev, group, RLEN, HD), jnp.float32),
    )
    self_scores = (
        jnp.einsum(
            "rtkgd,rnkd->rkgtn", heads_q, own_rows[:, :, :, 0], preferred_element_type=jnp.float32
        )
        * scale
    )
    state = absorb(
        state, self_scores, own_mask[:, None, None], own_rows[:, :, :, 1], "rkgtn,rnkd->rkgtd"
    )
    gathered = lax.all_gather(prompt_kv, ("resp", "tensor"), axis=0, tiled=True)
    column = lax.axis_index("tensor") * (kv_dev * 2 * HD)
    prompt_rows = lax.dynamic_slice_in_dim(gathered, column, kv_dev * 2 * HD, 1)
    prompt_count = prompt_rows.shape[0] // PLEN
    blocks = prompt_rows.reshape(prompt_count, PLEN, kv_dev, 2, HD)

    def visit(inner, packed):
        keys_block, which = packed
        mask = (my_groups == which)[:, None, None, None, None]
        scores = (
            jnp.einsum(
                "rtkgd,nkd->rkgtn", heads_q, keys_block[:, :, 0], preferred_element_type=jnp.float32
            )
            * scale
        )
        inner = absorb(inner, scores, mask, keys_block[:, :, 1], "rkgtn,nkd->rkgtd")
        return (inner, None)

    numbers = jnp.arange(prompt_count, dtype=jnp.int32)
    state, unused = lax.scan(visit, state, (blocks, numbers))
    top, total, acc = state
    out = (acc / total[..., None]).transpose(0, 3, 1, 2, 4)
    live = slots[None, :] < my_lengths[:, None]
    out = jnp.where(live[:, :, None, None, None], out, 0.0)
    return out.reshape(RESP_DEV * RLEN, kv_dev * group * HD).astype(jnp.bfloat16)


def solution(mesh):
    placed = (
        P(("dp", "resp"), "tensor"),
        P(("dp", "resp", "tensor"), None),
        P(("dp", "resp", "tensor"), None),
        P("dp"),
        P("dp"),
        P("dp", None),
    )
    return jax.shard_map(
        local, mesh=mesh, in_specs=placed, out_specs=P(("dp", "resp"), "tensor"), check_vma=False
    )
```

profile of v0, /device:TPU:0, one launch (start us, length us, event | category | flops | bytes accessed | tf_op | source)
XLA Modules:
  0.0 1366.4 jit_solution(1070069536699136868)
XLA Ops:
  7.3 1.7 copy.99
  8.9 3.5 all-to-all-start
  15.2 1.8 reshape.306
  17.0 1.7 reshape.304
  19.1 148.1 %gather_fusion = pred[16384,4]{1,0:T(8,128)(4,1)} fusion(pred[4,4,4]{0,2,1:T(4,128)(4,1)S(1)} %or.49, s32[16384]{0:T(1024)S(1)} %or_bitcast_fusion), kind=kCustom, calls=%fused_computation | custom fusion | bytes 262144 | tf_op jit(solution)/shard_map/gather | solution.py:60
  167.2 6.4 copy.50
  174.2 1.6 select_reduce_fusion
  175.9 1.8 fusion.17
  177.7 1.7 copy.59
  179.7 1141.6 %all-gather.2.cloned.1.call-done = bf16[2048,2048]{1,0:T(8,128)(2,1)} async-done(((bf16[8,2048]{1,0:T(8,128)(2,1)}), bf16[2048,2048]{1,0:T(8,128)(2,1)}) %all-gather.2.cloned.1.call-update) | async-done | bytes 8388624 | tf_op jit(solution)/shard_map/all_gather | solution.py:76
  1321.4 1.3 constant_dynamic-slice_fusion.1
  1322.7 1.1 reshape.305
  1323.8 33.9 %while.14 = (s32[]{:T(128)}, f32[4,1,5,128]{3,2,0,1:T(8,128)S(1)}, f32[4,1,5,128]{3,2,0,1:T(8,128)S(1)}, f32[4,1,5,128,128]{3,4,2,0,1:T(8,128)S(1)}, s32[8]{0:T(...) while((s32[]{:T(128)}, f32[4,1,5,128]{3,2,0,1:T(8,128)S(1)}, ...), condition=%wide.region_9.10_spmd, body=%wide.region_6.9_spmd.sunk | while | flops 343416320 | bytes 11973777 | solution.py:95
  1325.0 1.0 constant_dynamic-slice_fusion.4
  1329.3 1.0 constant_dynamic-slice_fusion.4
  1333.5 1.0 constant_dynamic-slice_fusion.4
  1337.8 1.0 constant_dynamic-slice_fusion.4
  1339.9 0.8 fusion.45
  1342.0 1.0 constant_dynamic-slice_fusion.4
  1346.3 1.0 constant_dynamic-slice_fusion.4
  1350.5 1.0 constant_dynamic-slice_fusion.4
  1354.7 1.0 constant_dynamic-slice_fusion.4
  1356.9 0.8 fusion.45
  1358.6 0.9 copy.98
  (115 shorter events, 29.1 us)
Async XLA Ops:
  6.5 6.7 copy-start
  6.5 10.4 copy-start.1
  6.5 1314.8 %all-gather.2.cloned.1.call-start = ((), (), s32[]{:S(2)}) async-start(), calls=%async_computation.1 | async-start | bytes 8421376 | tf_op jit(solution)/shard_map/all_gather | solution.py:76
  8.9 9.8 copy-start.2
  8.9 164.8 %all-to-all-start = ((bf16[64,8,256]{2,0,1:T(8,128)(2,1)}), bf16[64,8,256]{2,0,1:T(8,128)(2,1)S(1)}, u32[]{:S(2)}, u32[]{:S(2)}) async-start(bf16[64,8,256]{2,0,1:T(8,128)(2,1)} %bitcast.106), calls=%async_computation | async-start | bytes 524288 | tf_op jit(solution)/shard_map/all_to_all | solution.py:54
Sparse Core Ops, SparseCore 0:
  9.4 1311.8 all-gather.1
where the time goes:
time: 1370 us
  waiting for transfers between devices  1140 us (83%)
  local copies, waits for them, and re-layouts  181 us (13%)
  matrix products  14.1 us (1%)
    all_gather x1, waiting for transfers between devices, local(): gathered = lax.all_gather(prompt_kv, ('resp', 'tensor'), axis=0, tiled=True)  1140 us
    gather x2, local copies, waits for them, and re-layouts, local(): seen = sight[:, block_of[:, None], block_of[None, :]]  155 us
  transfers between devices with their start and end apart: 2, of which 1 were waited for; matrix products, arithmetic and copies ran while one was open for 12% of the time, Pallas kernels for 0%

commit v1 on v0

v1 whole, which is shorter than its diff:
```python
import functools
import math

import jax
import jax.numpy as jnp
from jax import lax
from jax.experimental import pallas as pl
from jax.experimental.pallas import tpu as pltpu
from jax.sharding import PartitionSpec as P

H = 40
KVH = 8
HD = 128
RLEN = 128
NB = 4
PLEN = 256
GROUP = H // KVH
RESP_DEV = 4
WIDTH = RLEN // NB
NZ = 16
SLOTS = 16
LINE = 8
NEG = -1e30
C2 = math.log2(math.e) / math.sqrt(HD)
MESH = pl.DeviceIdType.MESH
STEPS = (((0, 3), (0, 1)), ((3, 6), (3, 4), (3, 2)), ((6, 8), (6, 7), (6, 5)))
REACH = sorted({c - p for step in STEPS for p, c in step} | {p - c for step in STEPS for p, c in step})


def half(kv, sign, c):
    return c != 8 or (sign == 1) == (kv == 0)


def own_mask(first, j, lengths, parents):
    length = lengths[first + j]
    p2 = parents[2, first + j]
    p3 = parents[3, first + j]
    s21 = p2 == 1
    s32 = p3 == 2
    s31 = (p3 == 1) | (s32 & s21)
    row = lax.broadcasted_iota(jnp.int32, (RLEN, RLEN), 0)
    col = lax.broadcasted_iota(jnp.int32, (RLEN, RLEN), 1)
    rb = row // WIDTH
    cb = col // WIDTH
    reach = jnp.where(rb == cb, row, -1)
    reach = jnp.where((cb == 0) & (rb > 0), RLEN, reach)
    reach = jnp.where((cb == 1) & (rb == 2), jnp.where(s21, RLEN, -1), reach)
    reach = jnp.where((cb == 1) & (rb == 3), jnp.where(s31, RLEN, -1), reach)
    reach = jnp.where((cb == 2) & (rb == 3), jnp.where(s32, RLEN, -1), reach)
    return (col <= reach) & (col < length)


def kernel(
    q_hbm, r_hbm, p_hbm, gids, lengths, parents, out_hbm,
    qs, kb, vb, rb, acc_s, m_s, p_s, obuf,
    lsem, asend, arecv, rsend, rrecv, zsend, zrecv, qsem, osem,
):
    resp = lax.axis_index("resp")
    t = lax.axis_index("tensor")
    z = resp // 2
    xh = resp % 2
    first = resp * RESP_DEV
    bufs = (kb, vb)

    def zz(o):
        return (z + o + NZ) % NZ

    def remote(src, dst, ss, rs, r, tt):
        return pltpu.make_async_remote_copy(
            src_ref=src, dst_ref=dst, send_sem=ss, recv_sem=rs,
            device_id={"resp": r, "tensor": tt}, device_id_type=MESH,
        )

    q_copy = pltpu.make_async_copy(q_hbm, qs, qsem)
    q_copy.start()

    peers = [(k // 8, k % 8) for k in range(1, SLOTS)]
    barrier = pltpu.get_barrier_semaphore()
    for o in REACH:
        pl.semaphore_signal(barrier, inc=1, device_id={"resp": zz(o) * 2 + xh, "tensor": t}, device_id_type=MESH)
    for dx, dt in peers:
        pl.semaphore_signal(
            barrier, inc=1, device_id={"resp": z * 2 + (xh + dx) % 2, "tensor": (t + dt) % 8}, device_id_type=MESH
        )
    pl.semaphore_wait(barrier, len(REACH) + len(peers))

    slot = xh * 8 + t

    def cols(tt, kv):
        return pl.ds(pl.multiple_of(tt * (2 * HD) + kv * HD, HD), HD)

    def pair(tt):
        return pl.ds(pl.multiple_of(tt * (2 * HD), 2 * HD), 2 * HD)

    def own_prompt(kv):
        return pltpu.make_async_copy(p_hbm.at[:, cols(t, kv)], bufs[kv].at[z, slot], lsem.at[kv])

    for kv in range(2):
        for dx, dt in peers:
            tt = (t + dt) % 8
            remote(
                p_hbm.at[:, cols(tt, kv)], bufs[kv].at[z, slot], asend.at[kv], arecv.at[kv], z * 2 + (xh + dx) % 2, tt
            ).start()
        own_prompt(kv).start()

    def own_rows():
        return pltpu.make_async_copy(r_hbm.at[:, pair(t)], rb.at[t], lsem.at[2])

    def rows_to(dt):
        tt = (t + dt) % 8
        return remote(r_hbm.at[:, pair(tt)], rb.at[t], rsend, rrecv, resp, tt)

    own_rows().start()
    for dt in range(1, 8):
        rows_to(dt).start()

    def hop(kv, sign, p, c):
        ref = bufs[kv].at[zz(-sign * p)]
        return remote(ref, ref, zsend.at[kv, sign % 3, c], zrecv.at[kv, sign % 3, c], zz(sign * (c - p)) * 2 + xh, t)

    started = []
    arrived = set()

    def arrive(kv, sign, c):
        if c == 0:
            sign = 0
        if (kv, sign, c) in arrived:
            return
        arrived.add((kv, sign, c))
        if c == 0:
            own_prompt(kv).wait()
            ref = bufs[kv].at[z, pl.ds(0, SLOTS - 1)]
            pltpu.make_async_copy(ref, ref, arecv.at[kv]).wait()
        else:
            hop(kv, sign, 0, c).wait_recv()

    def forward(kv, step):
        for p, c in STEPS[step]:
            for sign in (1, -1):
                if half(kv, sign, c):
                    arrive(kv, sign, p)
                    hop(kv, sign, p, c).start()
                    started.append((kv, sign, p, c))

    forward(0, 0)
    forward(1, 0)

    ref = rb.at[pl.ds(0, 7)]
    own_rows().wait()
    pltpu.make_async_copy(ref, ref, rrecv).wait()
    q_copy.wait()
    ones = jnp.ones((RLEN, HD), jnp.bfloat16)

    def own_part(j, carry):
        rows = rb[pl.ds(2 * j, 2)].reshape(RLEN, 2 * HD)
        keys = rows[:, :HD]
        values = jnp.concatenate([rows[:, HD:], ones], axis=1)
        mask = own_mask(first, j, lengths, parents)
        for g in range(GROUP):
            query = qs[pl.ds(j * RLEN, RLEN), g * HD : (g + 1) * HD]
            s = lax.dot_general(query, keys, (((1,), (1,)), ((), ())), preferred_element_type=jnp.float32)
            s = jnp.where(mask, s, NEG)
            m = jnp.max(s, axis=1, keepdims=True)
            e = jnp.exp2(s * C2 - m * C2).astype(jnp.bfloat16)
            acc_s[j, g] = jnp.dot(e, values, preferred_element_type=jnp.float32)
            m_s[j, g] = jnp.broadcast_to(m, (RLEN, HD))
        return carry

    lax.fori_loop(0, RESP_DEV, own_part, 0)

    forward(0, 1)
    forward(1, 1)
    forward(0, 2)
    forward(1, 2)

    for kv, sign, p, c in started:
        if kv == 0:
            arrive(kv, sign, c)

    def chosen(buf, j):
        gid = gids[first + j]
        rows = buf[pl.ds(2 * gid, 2)]
        return rows.astype(jnp.float32).reshape(PLEN, HD).astype(jnp.bfloat16)

    def prompt_keys(j, carry):
        keys = chosen(kb, j)
        for g in range(GROUP):
            query = qs[pl.ds(j * RLEN, RLEN), g * HD : (g + 1) * HD]
            s = lax.dot_general(query, keys, (((1,), (1,)), ((), ())), preferred_element_type=jnp.float32)
            m_own = m_s[j, g]
            m = jnp.maximum(m_own, jnp.max(s, axis=1, keepdims=True))
            mc = m * C2
            factor = jnp.exp2(m_own * C2 - mc)
            acc_s[j, g] = acc_s[j, g] * jnp.concatenate([factor, factor], axis=1)
            e = jnp.exp2(s * C2 - jnp.concatenate([mc, mc], axis=1))
            p_s[j, g] = e.astype(jnp.bfloat16)
        return carry

    lax.fori_loop(0, RESP_DEV, prompt_keys, 0)

    for kv, sign, p, c in started:
        if kv == 1:
            arrive(kv, sign, c)

    wide = jnp.ones((PLEN, HD), jnp.bfloat16)

    def prompt_values(j, carry):
        values = jnp.concatenate([chosen(vb, j), wide], axis=1)
        live = lax.broadcasted_iota(jnp.int32, (RLEN, HD), 0) < lengths[first + j]
        for g in range(GROUP):
            acc = acc_s[j, g] + jnp.dot(p_s[j, g], values, preferred_element_type=jnp.float32)
            o = jnp.where(live, acc[:, :HD] / acc[:, HD:], 0.0)
            obuf[pl.ds(j * RLEN, RLEN), g * HD : (g + 1) * HD] = o.astype(jnp.bfloat16)
        return carry

    lax.fori_loop(0, RESP_DEV, prompt_values, 0)
    o_copy = pltpu.make_async_copy(obuf, out_hbm, osem)
    o_copy.start()

    for kv, sign, p, c in started:
        hop(kv, sign, p, c).wait_send()
    for kv in range(2):
        ref = bufs[kv].at[z, pl.ds(0, SLOTS - 1)]
        pltpu.make_async_copy(ref, ref, asend.at[kv]).wait()
    ref = rb.at[pl.ds(0, 7)]
    pltpu.make_async_copy(ref, ref, rsend).wait()
    o_copy.wait()


def local(queries, response_kv, prompt_kv, group_ids, lengths, tree_parent):
    dma = pltpu.SemaphoreType.DMA
    anywhere = pl.BlockSpec(memory_space=pl.ANY)
    scalars = pl.BlockSpec(memory_space=pltpu.SMEM)
    return pl.pallas_call(
        kernel,
        out_shape=jax.ShapeDtypeStruct(queries.shape, jnp.bfloat16),
        in_specs=[anywhere, anywhere, anywhere, scalars, scalars, scalars],
        out_specs=anywhere,
        scratch_shapes=[
            pltpu.VMEM((RESP_DEV * RLEN, GROUP * HD), jnp.bfloat16),
            pltpu.VMEM((NZ, SLOTS, LINE, HD), jnp.bfloat16),
            pltpu.VMEM((NZ, SLOTS, LINE, HD), jnp.bfloat16),
            pltpu.VMEM((8, 64, 2 * HD), jnp.bfloat16),
            pltpu.VMEM((RESP_DEV, GROUP, RLEN, 2 * HD), jnp.float32),
            pltpu.VMEM((RESP_DEV, GROUP, RLEN, HD), jnp.float32),
            pltpu.VMEM((RESP_DEV, GROUP, RLEN, PLEN), jnp.bfloat16),
            pltpu.VMEM((RESP_DEV * RLEN, GROUP * HD), jnp.bfloat16),
            dma((3,)), dma((2,)), dma((2,)), dma, dma, dma((2, 3, 9)), dma((2, 3, 9)), dma, dma,
        ],
        compiler_params=pltpu.CompilerParams(
            collective_id=0, has_side_effects=True, vmem_limit_bytes=60 << 20
        ),
        cost_estimate=pl.CostEstimate(flops=1 << 29, bytes_accessed=3 << 20, transcendentals=1 << 20),
    )(queries, response_kv, prompt_kv, group_ids, lengths, tree_parent.T)


def solution(mesh):
    placed = (
        P(("dp", "resp"), "tensor"),
        P(("dp", "resp", "tensor"), None),
        P(("dp", "resp", "tensor"), None),
        P("dp"),
        P("dp"),
        P("dp", None),
    )
    return jax.shard_map(
        local, mesh=mesh, in_specs=placed, out_specs=P(("dp", "resp"), "tensor"), check_vma=False
    )
```

time: 1370 us -> 45.1 us (0.03)
  the two profiles are of different devices: /device:TPU:0 before, /device:TPU:1 now
where the time goes in v1:
time: 45.1 us; the launch traced here: 44.8 us
  Pallas kernels  42.8 us (95%)
  local copies, waits for them, and re-layouts  1.98 us (4%)
    pallas_call x1, Pallas kernels, local(): pl.pallas_call(kernel, out_shape=jax.ShapeDtypeStruct(queries.shape, jnp....  42.8 us
    unnamed x1, local copies, waits for them, and re-layouts  1.98 us

profile of v1, /device:TPU:1, one launch (start us, length us, event | category | flops | bytes accessed | tf_op | source)
XLA Modules:
  0.0 44.8 jit_solution(5015077781113273242)
XLA Ops:
  0.0 42.8 %shard_map.64 = bf16[512,640]{1,0:T(8,128)(2,1)} custom-call(bf16[512,640]{1,0:T(8,128)(2,1)} %q_hbm.1, bf16[64,2048]{1,0:T(8,128)(2,1)} %r_hbm.1, bf16[8,2048]{1,0:T(8,128)(2,1)} %p_hbm.1, s32[128]{0:T(128)} %gids.1, s32[128]{0:T(128)} %lengths.1, s32[4,128]{1,0:T(4,128)} %bitcast.1), custom_call_target="tpu_custom_call" | custom-call | flops 536870912 | bytes 3145728 | tf_op jit(solution)/shard_map/pallas_call | solution.py:234
  42.8 2.0 %copy.8 = bf16[512,640]{1,0:T(8,128)(2,1)} copy(bf16[512,640]{1,0:T(8,128)(2,1)} %shard_map.64) | data formatting | bytes 1310720

commit v2 on v1

v2 whole, which is shorter than its diff:
```python
import math

import jax
import jax.numpy as jnp
from jax import lax
from jax.experimental import pallas as pl
from jax.experimental.pallas import tpu as pltpu
from jax.sharding import PartitionSpec as P

H = 40
KVH = 8
HD = 128
RLEN = 128
NB = 4
PLEN = 256
RESPONSES = 128
GROUP = H // KVH
RESP_DEV = 4
NZ = 16
SLOTS = 16
LINE = 8
NEG = -1e30
C2 = math.log2(math.e) / math.sqrt(HD)
MESH = pl.DeviceIdType.MESH
STEPS = (((0, 3),), ((3, 6),))
AHEAD = 6
NEAR = (3, -3, 2, -2, 1, -1)


def own_mask(first, j, lengths, parents):
    length = lengths[first + j]
    p2 = parents[2, first + j]
    p3 = parents[3, first + j]
    s21 = p2 == 1
    s32 = p3 == 2
    s31 = (p3 == 1) | (s32 & s21)
    row = lax.broadcasted_iota(jnp.int32, (RLEN, RLEN), 0)
    col = lax.broadcasted_iota(jnp.int32, (RLEN, RLEN), 1)
    rb = row >> 5
    cb = col >> 5
    reach = jnp.where(rb == cb, row, -1)
    reach = jnp.where((cb == 0) & (rb > 0), RLEN, reach)
    reach = jnp.where((cb == 1) & (rb == 2), jnp.where(s21, RLEN, -1), reach)
    reach = jnp.where((cb == 1) & (rb == 3), jnp.where(s31, RLEN, -1), reach)
    reach = jnp.where((cb == 2) & (rb == 3), jnp.where(s32, RLEN, -1), reach)
    return (col <= reach) & (col < length)


def kernel(
    q_hbm, r_hbm, p_hbm, g_hbm, l_hbm, t_hbm, obuf,
    gids, lengths, parents, qs, raw, prompts, rb, acc_s, m_s,
    psend, precv, rsend, rrecv, zsend, zrecv, qsem, ssem, lsem, ready,
):
    resp = lax.axis_index("resp")
    t = lax.axis_index("tensor")
    z = resp // 2
    xh = resp % 2
    first = resp * RESP_DEV
    slot = xh * 8 + t

    def zz(o):
        return (z + o + NZ) % NZ

    def place(r, tt):
        return {"resp": r, "tensor": tt}

    def remote(src, dst, ss, rs, r, tt):
        return pltpu.make_async_remote_copy(
            src_ref=src, dst_ref=dst, send_sem=ss, recv_sem=rs, device_id=place(r, tt), device_id_type=MESH
        )

    peers = sorted(
        ((k // 8, k % 8) for k in range(1, SLOTS)), key=lambda p: (-2 * p[0] - min(p[1] // 2, 4 - p[1] // 2) - p[1] % 2, p)
    )

    def greet(sem, r, tt):
        pl.semaphore_signal(sem, inc=1, device_id=place(r, tt), device_id_type=MESH)

    barrier = pltpu.get_barrier_semaphore()
    for o in NEAR:
        greet(barrier, zz(o) * 2 + xh, t)
    for dx, dt in peers:
        greet(barrier, z * 2 + (xh + dx) % 2, (t + dt) % 8)

    own_raw = pltpu.make_async_copy(p_hbm, raw.at[z], lsem)
    own_raw.start()
    small = [
        pltpu.make_async_copy(src, dst, ssem.at[i])
        for i, (src, dst) in enumerate(((g_hbm, gids), (l_hbm, lengths), (t_hbm, parents)))
    ]
    for copy in small:
        copy.start()
    q_copy = pltpu.make_async_copy(q_hbm, qs, qsem)
    q_copy.start()

    own_raw.wait()
    pl.semaphore_wait(barrier, len(NEAR) + len(peers))

    def pair(tt):
        return pl.ds(pl.multiple_of(tt * (2 * HD), 2 * HD), 2 * HD)

    started = []
    here = set()
    waiting = []

    def hop(sign, p, c):
        ref = raw.at[zz(-sign * p)]
        return remote(ref, ref, zsend.at[sign % 3, c], zrecv.at[sign % 3, c], zz(sign * (c - p)) * 2 + xh, t)

    def arrive(sign, c):
        sign = sign if c else 0
        if (sign, c) not in here:
            here.add((sign, c))
            if c:
                hop(sign, 0, c).wait_recv()
            waiting.append((sign, c))

    def forward(step):
        for p, c in STEPS[step]:
            for sign in (1, -1):
                if c != 8 or sign == 1:
                    arrive(sign, p)
                    hop(sign, p, c).start()
                    started.append((sign, p, c))

    spread_count = [0]

    def to_plane(src, o, half=None):
        targets = peers if o == 0 else peers + [(0, 0)]
        for dx, dt in targets:
            if half is not None and dx:
                continue
            tt = (t + dt) % 8
            r = zz(o) * 2 + (half if half is not None else (xh + dx) % 2)
            remote(raw.at[src, :, pair(tt)], prompts.at[src, slot], psend, precv, r, tt).start()
            spread_count[0] += 1
        if o == 0:
            pltpu.make_async_copy(raw.at[src, :, pair(t)], prompts.at[src, slot], precv).start()

    def spread():
        while waiting:
            sign, c = waiting.pop(0)
            src = zz(-sign * c)
            if c == AHEAD:
                to_plane(src, 2 * sign, 0 if sign == 1 else 1)
            to_plane(src, 1)
            to_plane(src, -1)
            to_plane(src, 0)

    arrive(0, 0)
    forward(0)
    for dx, dt in peers:
        greet(ready, z * 2 + (xh + dx) % 2, (t + dt) % 8)
    waiting.clear()
    to_plane(z, 0)

    pltpu.make_async_copy(r_hbm.at[:, pair(t)], rb.at[t], rrecv).start()
    for dt in range(1, 8):
        tt = (t + dt) % 8
        remote(r_hbm.at[:, pair(tt)], rb.at[t], rsend, rrecv, resp, tt).start()

    pl.semaphore_wait(ready, len(peers))
    to_plane(z, 1)
    to_plane(z, -1)

    for copy in small:
        copy.wait()
    q_copy.wait()

    def stacked(j):
        rows = qs[pl.ds(j * RLEN, RLEN), :]
        return jnp.concatenate([rows[:, g * HD : (g + 1) * HD] for g in range(GROUP)], axis=0)

    def own_part(j, carry):
        rows = rb[pl.ds(2 * j, 2)].reshape(RLEN, 2 * HD)
        keys = rows[:, :HD]
        values = jnp.concatenate([rows[:, HD:], jnp.ones((RLEN, HD), jnp.bfloat16)], axis=1)
        bias = jnp.where(own_mask(first, j, lengths, parents), 0.0, NEG)
        s = lax.dot_general(stacked(j), keys, (((1,), (1,)), ((), ())), preferred_element_type=jnp.float32)
        s = s + jnp.concatenate([bias] * GROUP, axis=0)
        m = jnp.max(s, axis=1, keepdims=True)
        e = jnp.exp2(s * C2 - m * C2).astype(jnp.bfloat16)
        acc_s[j] = jnp.dot(e, values, preferred_element_type=jnp.float32)
        m_s[j] = jnp.broadcast_to(m, (GROUP * RLEN, HD))
        return carry

    def own():
        pltpu.make_async_copy(rb, rb, rrecv).wait()
        lax.fori_loop(0, RESP_DEV, own_part, 0)

    for step in range(1, len(STEPS)):
        forward(step)
        spread()
    for sign, p, c in started:
        arrive(sign, c)
        spread()
    own()
    pltpu.make_async_copy(prompts, prompts, precv).wait()

    def chosen(j, at):
        rows = prompts[pl.ds(2 * gids[first + j], 2), :, :, at : at + HD]
        return rows.astype(jnp.float32).reshape(PLEN, HD).astype(jnp.bfloat16)

    def prompt_part(j, carry):
        s = lax.dot_general(stacked(j), chosen(j, 0), (((1,), (1,)), ((), ())), preferred_element_type=jnp.float32)
        m_own = m_s[j]
        m = jnp.maximum(m_own, jnp.max(s, axis=1, keepdims=True))
        mc = m * C2
        factor = jnp.exp2(m_own * C2 - mc)
        e = jnp.exp2(s * C2 - jnp.concatenate([mc, mc], axis=1)).astype(jnp.bfloat16)
        values = jnp.concatenate([chosen(j, HD), jnp.ones((PLEN, HD), jnp.bfloat16)], axis=1)
        acc = acc_s[j] * jnp.concatenate([factor, factor], axis=1)
        acc = acc + jnp.dot(e, values, preferred_element_type=jnp.float32)
        o = acc[:, :HD] / acc[:, HD:]
        live = lax.broadcasted_iota(jnp.int32, (RLEN, HD), 0) < lengths[first + j]
        for g in range(GROUP):
            part = jnp.where(live, o[g * RLEN : (g + 1) * RLEN], 0.0)
            obuf[pl.ds(j * RLEN, RLEN), g * HD : (g + 1) * HD] = part.astype(jnp.bfloat16)
        return carry

    lax.fori_loop(0, RESP_DEV, prompt_part, 0)
    for sign, p, c in started:
        hop(sign, p, c).wait_send()
    left = spread_count[0]
    while left:
        n = min(left, NZ * SLOTS)
        left -= n
        if n >= SLOTS:
            pltpu.make_async_copy(
                prompts.at[pl.ds(0, n // SLOTS)], prompts.at[pl.ds(0, n // SLOTS)], psend
            ).wait()
        if n % SLOTS:
            ref = prompts.at[0, pl.ds(0, n % SLOTS)]
            pltpu.make_async_copy(ref, ref, psend).wait()
    ref = rb.at[pl.ds(0, 7)]
    pltpu.make_async_copy(ref, ref, rsend).wait()


def store(src, dst, sem):
    copy = pltpu.make_async_copy(src, dst, sem)
    copy.start()
    copy.wait()


def local(queries, response_kv, prompt_kv, group_ids, lengths, tree_parent):
    dma = pltpu.SemaphoreType.DMA
    anywhere = pl.BlockSpec(memory_space=pl.ANY)
    attended = pl.pallas_call(
        kernel,
        out_shape=pltpu.VMEM(queries.shape, jnp.bfloat16),
        in_specs=[anywhere] * 6,
        out_specs=pl.BlockSpec(memory_space=pltpu.VMEM),
        scratch_shapes=[
            pltpu.SMEM((RESPONSES,), jnp.int32),
            pltpu.SMEM((RESPONSES,), jnp.int32),
            pltpu.SMEM((NB, RESPONSES), jnp.int32),
            pltpu.VMEM((RESP_DEV * RLEN, GROUP * HD), jnp.bfloat16),
            pltpu.VMEM((NZ, LINE, KVH * 2 * HD), jnp.bfloat16),
            pltpu.VMEM((NZ, SLOTS, LINE, 2 * HD), jnp.bfloat16),
            pltpu.VMEM((8, 64, 2 * HD), jnp.bfloat16),
            pltpu.VMEM((RESP_DEV, GROUP * RLEN, 2 * HD), jnp.float32),
            pltpu.VMEM((RESP_DEV, GROUP * RLEN, HD), jnp.float32),
            dma, dma, dma, dma, dma((3, 9)), dma((3, 9)), dma, dma((3,)), dma, pltpu.SemaphoreType.REGULAR,
        ],
        compiler_params=pltpu.CompilerParams(
            collective_id=0, has_side_effects=True, vmem_limit_bytes=60 << 20
        ),
        cost_estimate=pl.CostEstimate(flops=1 << 29, bytes_accessed=3 << 20, transcendentals=1 << 20),
    )(queries, response_kv, prompt_kv, group_ids, lengths, tree_parent.T)
    return pl.pallas_call(
        store,
        out_shape=jax.ShapeDtypeStruct(queries.shape, jnp.bfloat16),
        in_specs=[pl.BlockSpec(memory_space=pltpu.VMEM)],
        out_specs=anywhere,
        scratch_shapes=[dma],
        compiler_params=pltpu.CompilerParams(vmem_limit_bytes=2 << 20),
    )(attended)


def solution(mesh):
    placed = (
        P(("dp", "resp"), "tensor"),
        P(("dp", "resp", "tensor"), None),
        P(("dp", "resp", "tensor"), None),
        P("dp"),
        P("dp"),
        P("dp", None),
    )
    return jax.shard_map(
        local, mesh=mesh, in_specs=placed, out_specs=P(("dp", "resp"), "tensor"), check_vma=False
    )
```

time: 45.1 us -> 35.4 us (0.78)
  Pallas kernels: 42.8 us -> 35.3 us
  local copies, waits for them, and re-layouts: 1.98 us -> 0 us
    pallas_call x1 -> x2, Pallas kernels: 42.8 us -> 35.3 us  [the longest x1 34.4 us: local(): pl.pallas_call(kernel, out_shape=pltpu.VMEM(queries.shape, jnp.bfloat16),...]
    unnamed x1 -> x0, local copies, waits for them, and re-layouts: 1.98 us -> none
where the time goes in v2:
time: 35.4 us; the launch traced here: 35.3 us
  Pallas kernels  35.3 us (100%)
    pallas_call x1, Pallas kernels, local(): pl.pallas_call(kernel, out_shape=pltpu.VMEM(queries.shape, jnp.bfloat16),...  34.4 us
    pallas_call x1, Pallas kernels, local(): pl.pallas_call(store, out_shape=jax.ShapeDtypeStruct(queries.shape, jnp.b...  0.85 us

profile of v2, /device:TPU:1, one launch (start us, length us, event | category | flops | bytes accessed | tf_op | source)
XLA Modules:
  0.0 35.3 jit_solution(7040767052846047468)
XLA Ops:
  0.0 34.4 %shard_map.64.src = bf16[512,640]{1,0:T(8,128)(2,1)S(1)} custom-call(bf16[512,640]{1,0:T(8,128)(2,1)} %q_hbm.1, bf16[64,2048]{1,0:T(8,128)(2,1)} %r_hbm.1, bf16[8,2048]{1,0:T(8,128)(2,1)} %p_hbm.1, s32[128]{0:T(128)} %g_hbm.1, s32[128]{0:T(128)} %l_hbm.1, s32[4,128]{1,0:T(4,128)} %bitcast.1), custom_call_target="tpu_custom_call" | custom-call | flops 536870912 | bytes 3145728 | tf_op jit(solution)/shard_map/pallas_call | solution.py:248
  34.4 0.8 %shard_map.65 = bf16[512,640]{1,0:T(8,128)(2,1)} custom-call(bf16[512,640]{1,0:T(8,128)(2,1)S(1)} %shard_map.64.src), custom_call_target="tpu_custom_call" | custom-call | tf_op jit(solution)/shard_map/pallas_call | solution.py:270

commit v3 on v2

--- a/solution.py
+++ b/solution.py
@@ -22,8 +22,6 @@
 NEG = -1e30
 C2 = math.log2(math.e) / math.sqrt(HD)
 MESH = pl.DeviceIdType.MESH
-STEPS = (((0, 3),), ((3, 6),))
-AHEAD = 6
 NEAR = (3, -3, 2, -2, 1, -1)
 
 
@@ -48,7 +46,7 @@
 
 def kernel(
     q_hbm, r_hbm, p_hbm, g_hbm, l_hbm, t_hbm, obuf,
-    gids, lengths, parents, qs, raw, prompts, rb, acc_s, m_s,
+    gids, lengths, parents, qs, kr, vr, kb, vb, rb, acc_s, m_s, p_s,
     psend, precv, rsend, rrecv, zsend, zrecv, qsem, ssem, lsem, ready,
 ):
     resp = lax.axis_index("resp")
@@ -82,8 +80,12 @@
     for dx, dt in peers:
         greet(barrier, z * 2 + (xh + dx) % 2, (t + dt) % 8)
 
-    own_raw = pltpu.make_async_copy(p_hbm, raw.at[z], lsem)
-    own_raw.start()
+    raws = (kr, vr)
+    for kv in range(2):
+        for h in range(KVH):
+            pltpu.make_async_copy(
+                p_hbm.at[:, pl.ds((2 * h + kv) * HD, HD)], raws[kv].at[z, :, pl.ds(h * HD, HD)], lsem.at[kv]
+            ).start()
     small = [
         pltpu.make_async_copy(src, dst, ssem.at[i])
         for i, (src, dst) in enumerate(((g_hbm, gids), (l_hbm, lengths), (t_hbm, parents)))
@@ -93,65 +95,57 @@
     q_copy = pltpu.make_async_copy(q_hbm, qs, qsem)
     q_copy.start()
 
-    own_raw.wait()
+    for kv in range(2):
+        pltpu.make_async_copy(raws[kv].at[z], raws[kv].at[z], lsem.at[kv]).wait()
     pl.semaphore_wait(barrier, len(NEAR) + len(peers))
 
     def pair(tt):
         return pl.ds(pl.multiple_of(tt * (2 * HD), 2 * HD), 2 * HD)
 
-    started = []
-    here = set()
-    waiting = []
-
-    def hop(sign, p, c):
-        ref = raw.at[zz(-sign * p)]
-        return remote(ref, ref, zsend.at[sign % 3, c], zrecv.at[sign % 3, c], zz(sign * (c - p)) * 2 + xh, t)
-
-    def arrive(sign, c):
-        sign = sign if c else 0
-        if (sign, c) not in here:
-            here.add((sign, c))
-            if c:
-                hop(sign, 0, c).wait_recv()
-            waiting.append((sign, c))
-
-    def forward(step):
-        for p, c in STEPS[step]:
-            for sign in (1, -1):
-                if c != 8 or sign == 1:
-                    arrive(sign, p)
-                    hop(sign, p, c).start()
-                    started.append((sign, p, c))
+    def hop(kv, sign, p, c):
+        ref = raws[kv].at[zz(-sign * p)]
+        return remote(
+            ref, ref, zsend.at[kv, sign % 3, c], zrecv.at[kv, sign % 3, c], zz(sign * (c - p)) * 2 + xh, t
+        )
+
+    def forward(kv, p, c):
+        for sign in (1, -1):
+            if p:
+                hop(kv, sign, 0, p).wait_recv()
+            hop(kv, sign, p, c).start()
 
     spread_count = [0]
 
-    def to_plane(src, o, half=None):
+    def column(tt):
+        return pl.ds(pl.multiple_of(tt * HD, HD), HD)
+
+    def to_plane(src, o, half=None, kvs=(0, 1)):
         targets = peers if o == 0 else peers + [(0, 0)]
-        for dx, dt in targets:
-            if half is not None and dx:
-                continue
-            tt = (t + dt) % 8
-            r = zz(o) * 2 + (half if half is not None else (xh + dx) % 2)
-            remote(raw.at[src, :, pair(tt)], prompts.at[src, slot], psend, precv, r, tt).start()
-            spread_count[0] += 1
-        if o == 0:
-            pltpu.make_async_copy(raw.at[src, :, pair(t)], prompts.at[src, slot], precv).start()
-
-    def spread():
-        while waiting:
-            sign, c = waiting.pop(0)
-            src = zz(-sign * c)
-            if c == AHEAD:
-                to_plane(src, 2 * sign, 0 if sign == 1 else 1)
-            to_plane(src, 1)
-            to_plane(src, -1)
-            to_plane(src, 0)
-
-    arrive(0, 0)
-    forward(0)
+        for kv in kvs:
+            buf = (kb, vb)[kv]
+            for dx, dt in targets:
+                if half is not None and dx:
+                    continue
+                tt = (t + dt) % 8
+                r = zz(o) * 2 + (half if half is not None else (xh + dx) % 2)
+                remote(raws[kv].at[src, :, column(tt)], buf.at[src, slot], psend.at[kv], precv.at[kv], r, tt).start()
+                if kv == 0:
+                    spread_count[0] += 1
+            if o == 0:
+                pltpu.make_async_copy(raws[kv].at[src, :, column(t)], buf.at[src, slot], precv.at[kv]).start()
+
+    def spread(kv, c):
+        for sign in (1, -1):
+            src = zz(-c * sign)
+            if c == 6:
+                to_plane(src, 2 * sign, 0 if sign == 1 else 1, (kv,))
+            for o in (1, -1, 0):
+                to_plane(src, o, None, (kv,))
+
+    forward(0, 0, 3)
+    forward(1, 0, 3)
     for dx, dt in peers:
         greet(ready, z * 2 + (xh + dx) % 2, (t + dt) % 8)
-    waiting.clear()
     to_plane(z, 0)
 
     pltpu.make_async_copy(r_hbm.at[:, pair(t)], rb.at[t], rrecv).start()
@@ -186,31 +180,38 @@
 
     def own():
         pltpu.make_async_copy(rb, rb, rrecv).wait()
-        lax.fori_loop(0, RESP_DEV, own_part, 0)
-
-    for step in range(1, len(STEPS)):
-        forward(step)
-        spread()
-    for sign, p, c in started:
-        arrive(sign, c)
-        spread()
+        lax.fori_loop(0, RESP_DEV, own_part, 0, unroll=True)
+
+    forward(0, 3, 6)
+    forward(1, 3, 6)
+    spread(0, 3)
+    spread(1, 3)
+    for sign in (1, -1):
+        hop(0, sign, 0, 6).wait_recv()
+    spread(0, 6)
+    for sign in (1, -1):
+        hop(1, sign, 0, 6).wait_recv()
+    spread(1, 6)
     own()
-    pltpu.make_async_copy(prompts, prompts, precv).wait()
-
-    def chosen(j, at):
-        rows = prompts[pl.ds(2 * gids[first + j], 2), :, :, at : at + HD]
+    pltpu.make_async_copy(kb, kb, precv.at[0]).wait()
+
+    def chosen(buf, j):
+        rows = buf[pl.ds(2 * gids[first + j], 2)]
         return rows.astype(jnp.float32).reshape(PLEN, HD).astype(jnp.bfloat16)
 
-    def prompt_part(j, carry):
-        s = lax.dot_general(stacked(j), chosen(j, 0), (((1,), (1,)), ((), ())), preferred_element_type=jnp.float32)
+    def keys_part(j, carry):
+        s = lax.dot_general(stacked(j), chosen(kb, j), (((1,), (1,)), ((), ())), preferred_element_type=jnp.float32)
         m_own = m_s[j]
         m = jnp.maximum(m_own, jnp.max(s, axis=1, keepdims=True))
         mc = m * C2
         factor = jnp.exp2(m_own * C2 - mc)
-        e = jnp.exp2(s * C2 - jnp.concatenate([mc, mc], axis=1)).astype(jnp.bfloat16)
-        values = jnp.concatenate([chosen(j, HD), jnp.ones((PLEN, HD), jnp.bfloat16)], axis=1)
-        acc = acc_s[j] * jnp.concatenate([factor, factor], axis=1)
-        acc = acc + jnp.dot(e, values, preferred_element_type=jnp.float32)
+        acc_s[j] = acc_s[j] * jnp.concatenate([factor, factor], axis=1)
+        p_s[j] = jnp.exp2(s * C2 - jnp.concatenate([mc, mc], axis=1)).astype(jnp.bfloat16)
+        return carry
+
+    def values_part(j, carry):
+        values = jnp.concatenate([chosen(vb, j), jnp.ones((PLEN, HD), jnp.bfloat16)], axis=1)
+        acc = acc_s[j] + jnp.dot(p_s[j], values, preferred_element_type=jnp.float32)
         o = acc[:, :HD] / acc[:, HD:]
         live = lax.broadcasted_iota(jnp.int32, (RLEN, HD), 0) < lengths[first + j]
         for g in range(GROUP):
@@ -218,20 +219,24 @@
             obuf[pl.ds(j * RLEN, RLEN), g * HD : (g + 1) * HD] = part.astype(jnp.bfloat16)
         return carry
 
-    lax.fori_loop(0, RESP_DEV, prompt_part, 0)
-    for sign, p, c in started:
-        hop(sign, p, c).wait_send()
-    left = spread_count[0]
-    while left:
-        n = min(left, NZ * SLOTS)
-        left -= n
-        if n >= SLOTS:
-            pltpu.make_async_copy(
-                prompts.at[pl.ds(0, n // SLOTS)], prompts.at[pl.ds(0, n // SLOTS)], psend
-            ).wait()
-        if n % SLOTS:
-            ref = prompts.at[0, pl.ds(0, n % SLOTS)]
-            pltpu.make_async_copy(ref, ref, psend).wait()
+    lax.fori_loop(0, RESP_DEV, keys_part, 0, unroll=True)
+    pltpu.make_async_copy(vb, vb, precv.at[1]).wait()
+    lax.fori_loop(0, RESP_DEV, values_part, 0, unroll=True)
+    for kv in range(2):
+        for p, c in ((0, 3), (3, 6)):
+            for sign in (1, -1):
+                hop(kv, sign, p, c).wait_send()
+    for kv in range(2):
+        left = spread_count[0]
+        while left:
+            n = min(left, NZ * SLOTS)
+            left -= n
+            if n >= SLOTS:
+                ref = kb.at[pl.ds(0, n // SLOTS)]
+                pltpu.make_async_copy(ref, ref, psend.at[kv]).wait()
+            if n % SLOTS:
+                ref = kb.at[0, pl.ds(0, n % SLOTS)]
+                pltpu.make_async_copy(ref, ref, psend.at[kv]).wait()
     ref = rb.at[pl.ds(0, 7)]
     pltpu.make_async_copy(ref, ref, rsend).wait()
 
@@ -255,12 +260,15 @@
             pltpu.SMEM((RESPONSES,), jnp.int32),
             pltpu.SMEM((NB, RESPONSES), jnp.int32),
             pltpu.VMEM((RESP_DEV * RLEN, GROUP * HD), jnp.bfloat16),
-            pltpu.VMEM((NZ, LINE, KVH * 2 * HD), jnp.bfloat16),
-            pltpu.VMEM((NZ, SLOTS, LINE, 2 * HD), jnp.bfloat16),
+            pltpu.VMEM((NZ, LINE, KVH * HD), jnp.bfloat16),
+            pltpu.VMEM((NZ, LINE, KVH * HD), jnp.bfloat16),
+            pltpu.VMEM((NZ, SLOTS, LINE, HD), jnp.bfloat16),
+            pltpu.VMEM((NZ, SLOTS, LINE, HD), jnp.bfloat16),
             pltpu.VMEM((8, 64, 2 * HD), jnp.bfloat16),
             pltpu.VMEM((RESP_DEV, GROUP * RLEN, 2 * HD), jnp.float32),
             pltpu.VMEM((RESP_DEV, GROUP * RLEN, HD), jnp.float32),
-            dma, dma, dma, dma, dma((3, 9)), dma((3, 9)), dma, dma((3,)), dma, pltpu.SemaphoreType.REGULAR,
+            pltpu.VMEM((RESP_DEV, GROUP * RLEN, PLEN), jnp.bfloat16),
+            dma((2,)), dma((2,)), dma, dma, dma((2, 3, 9)), dma((2, 3, 9)), dma, dma((3,)), dma((2,)), pltpu.SemaphoreType.REGULAR,
         ],
         compiler_params=pltpu.CompilerParams(
             collective_id=0, has_side_effects=True, vmem_limit_bytes=60 << 20

time: 35.4 us -> 33.6 us (0.949)
  Pallas kernels: 35.3 us -> 33.5 us
    pallas_call x1, Pallas kernels: 34.4 us -> 32.6 us  [local(): pl.pallas_call(kernel, out_shape=pltpu.VMEM(queries.shape, jnp.bfloat16),...]
where the time goes in v3:
time: 33.6 us; the launch traced here: 33.5 us
  Pallas kernels  33.5 us (100%)
    pallas_call x1, Pallas kernels, local(): pl.pallas_call(kernel, out_shape=pltpu.VMEM(queries.shape, jnp.bfloat16),...  32.6 us
    pallas_call x1, Pallas kernels, local(): pl.pallas_call(store, out_shape=jax.ShapeDtypeStruct(queries.shape, jnp.b...  0.85 us

profile of v3, /device:TPU:1, one launch (start us, length us, event | category | flops | bytes accessed | tf_op | source)
XLA Modules:
  0.0 33.5 jit_solution(12870524139808581462)
XLA Ops:
  0.0 32.6 %shard_map.64.src = bf16[512,640]{1,0:T(8,128)(2,1)S(1)} custom-call(bf16[512,640]{1,0:T(8,128)(2,1)} %q_hbm.1, bf16[64,2048]{1,0:T(8,128)(2,1)} %r_hbm.1, bf16[8,2048]{1,0:T(8,128)(2,1)} %p_hbm.1, s32[128]{0:T(128)} %g_hbm.1, s32[128]{0:T(128)} %l_hbm.1, s32[4,128]{1,0:T(4,128)} %bitcast.1), custom_call_target="tpu_custom_call" | custom-call | flops 536870912 | bytes 3145728 | tf_op jit(solution)/shard_map/pallas_call | solution.py:253
  32.7 0.8 %shard_map.65 = bf16[512,640]{1,0:T(8,128)(2,1)} custom-call(bf16[512,640]{1,0:T(8,128)(2,1)S(1)} %shard_map.64.src), custom_call_target="tpu_custom_call" | custom-call | tf_op jit(solution)/shard_map/pallas_call | solution.py:278

commit v4 on v3

--- a/solution.py
+++ b/solution.py
@@ -45,8 +45,8 @@
 
 
 def kernel(
-    q_hbm, r_hbm, p_hbm, g_hbm, l_hbm, t_hbm, obuf,
-    gids, lengths, parents, qs, kr, vr, kb, vb, rb, acc_s, m_s, p_s,
+    q_hbm, r_hbm, p_hbm, g_hbm, l_hbm, t_hbm, acc_s, p_s, v_s,
+    gids, lengths, parents, qs, kr, vr, kb, vb, rb, m_s,
     psend, precv, rsend, rrecv, zsend, zrecv, qsem, ssem, lsem, ready,
 ):
     resp = lax.axis_index("resp")
@@ -203,25 +203,17 @@
         s = lax.dot_general(stacked(j), chosen(kb, j), (((1,), (1,)), ((), ())), preferred_element_type=jnp.float32)
         m_own = m_s[j]
         m = jnp.maximum(m_own, jnp.max(s, axis=1, keepdims=True))
-        mc = m * C2
+        live = lax.broadcasted_iota(jnp.int32, (RLEN, HD), 0) < lengths[first + j]
+        mc = m * C2 + jnp.concatenate([jnp.where(live, 0.0, -NEG)] * GROUP, axis=0)
         factor = jnp.exp2(m_own * C2 - mc)
         acc_s[j] = acc_s[j] * jnp.concatenate([factor, factor], axis=1)
         p_s[j] = jnp.exp2(s * C2 - jnp.concatenate([mc, mc], axis=1)).astype(jnp.bfloat16)
         return carry
 
-    def values_part(j, carry):
-        values = jnp.concatenate([chosen(vb, j), jnp.ones((PLEN, HD), jnp.bfloat16)], axis=1)
-        acc = acc_s[j] + jnp.dot(p_s[j], values, preferred_element_type=jnp.float32)
-        o = acc[:, :HD] / acc[:, HD:]
-        live = lax.broadcasted_iota(jnp.int32, (RLEN, HD), 0) < lengths[first + j]
-        for g in range(GROUP):
-            part = jnp.where(live, o[g * RLEN : (g + 1) * RLEN], 0.0)
-            obuf[pl.ds(j * RLEN, RLEN), g * HD : (g + 1) * HD] = part.astype(jnp.bfloat16)
-        return carry
-
     lax.fori_loop(0, RESP_DEV, keys_part, 0, unroll=True)
     pltpu.make_async_copy(vb, vb, precv.at[1]).wait()
-    lax.fori_loop(0, RESP_DEV, values_part, 0, unroll=True)
+    for j in range(RESP_DEV):
+        v_s[j] = chosen(vb, j)
     for kv in range(2):
         for p, c in ((0, 3), (3, 6)):
             for sign in (1, -1):
@@ -241,20 +233,34 @@
     pltpu.make_async_copy(ref, ref, rsend).wait()
 
 
-def store(src, dst, sem):
-    copy = pltpu.make_async_copy(src, dst, sem)
-    copy.start()
-    copy.wait()
+def weigh(own, weights, rows, out, buf, sem):
+    def copy(j):
+        part = pl.ds(j * RLEN, RLEN)
+        return pltpu.make_async_copy(buf.at[part], out.at[part], sem.at[j])
+
+    for j in range(RESP_DEV):
+        values = jnp.concatenate([rows[j], jnp.ones((PLEN, HD), jnp.bfloat16)], axis=1)
+        acc = own[j] + jnp.dot(weights[j], values, preferred_element_type=jnp.float32)
+        o = (acc[:, :HD] / jnp.maximum(acc[:, HD:], 1.0)).astype(jnp.bfloat16)
+        for g in range(GROUP):
+            buf[j * RLEN : (j + 1) * RLEN, g * HD : (g + 1) * HD] = o[g * RLEN : (g + 1) * RLEN]
+        copy(j).start()
+    for j in range(RESP_DEV):
+        copy(j).wait()
 
 
 def local(queries, response_kv, prompt_kv, group_ids, lengths, tree_parent):
     dma = pltpu.SemaphoreType.DMA
     anywhere = pl.BlockSpec(memory_space=pl.ANY)
-    attended = pl.pallas_call(
+    parts = pl.pallas_call(
         kernel,
-        out_shape=pltpu.VMEM(queries.shape, jnp.bfloat16),
+        out_shape=(
+            pltpu.VMEM((RESP_DEV, GROUP * RLEN, 2 * HD), jnp.float32),
+            pltpu.VMEM((RESP_DEV, GROUP * RLEN, PLEN), jnp.bfloat16),
+            pltpu.VMEM((RESP_DEV, PLEN, HD), jnp.bfloat16),
+        ),
         in_specs=[anywhere] * 6,
-        out_specs=pl.BlockSpec(memory_space=pltpu.VMEM),
+        out_specs=(pl.BlockSpec(memory_space=pltpu.VMEM),) * 3,
         scratch_shapes=[
             pltpu.SMEM((RESPONSES,), jnp.int32),
             pltpu.SMEM((RESPONSES,), jnp.int32),
@@ -265,24 +271,22 @@
             pltpu.VMEM((NZ, SLOTS, LINE, HD), jnp.bfloat16),
             pltpu.VMEM((NZ, SLOTS, LINE, HD), jnp.bfloat16),
             pltpu.VMEM((8, 64, 2 * HD), jnp.bfloat16),
-            pltpu.VMEM((RESP_DEV, GROUP * RLEN, 2 * HD), jnp.float32),
             pltpu.VMEM((RESP_DEV, GROUP * RLEN, HD), jnp.float32),
-            pltpu.VMEM((RESP_DEV, GROUP * RLEN, PLEN), jnp.bfloat16),
             dma((2,)), dma((2,)), dma, dma, dma((2, 3, 9)), dma((2, 3, 9)), dma, dma((3,)), dma((2,)), pltpu.SemaphoreType.REGULAR,
         ],
         compiler_params=pltpu.CompilerParams(
-            collective_id=0, has_side_effects=True, vmem_limit_bytes=60 << 20
+            collective_id=0, has_side_effects=True, vmem_limit_bytes=56 << 20
         ),
         cost_estimate=pl.CostEstimate(flops=1 << 29, bytes_accessed=3 << 20, transcendentals=1 << 20),
     )(queries, response_kv, prompt_kv, group_ids, lengths, tree_parent.T)
     return pl.pallas_call(
-        store,
+        weigh,
         out_shape=jax.ShapeDtypeStruct(queries.shape, jnp.bfloat16),
-        in_specs=[pl.BlockSpec(memory_space=pltpu.VMEM)],
+        in_specs=[pl.BlockSpec(memory_space=pltpu.VMEM)] * 3,
         out_specs=anywhere,
-        scratch_shapes=[dma],
-        compiler_params=pltpu.CompilerParams(vmem_limit_bytes=2 << 20),
-    )(attended)
+        scratch_shapes=[pltpu.VMEM(queries.shape, jnp.bfloat16), dma((RESP_DEV,))],
+        compiler_params=pltpu.CompilerParams(vmem_limit_bytes=8 << 20),
+    )(*parts)
 
 
 def solution(mesh):

time: 33.6 us -> 33.6 us (level)
  no operation moved by 1% of the time
where the time goes in v4:
time: 33.6 us; the launch traced here: 33.5 us
  Pallas kernels  33.5 us (100%)
    pallas_call x1, Pallas kernels, local(): pl.pallas_call(kernel, out_shape=(pltpu.VMEM((RESP_DEV, GROUP * RLEN, 2 *...  32.2 us
    pallas_call x1, Pallas kernels, local(): pl.pallas_call(weigh, out_shape=jax.ShapeDtypeStruct(queries.shape, jnp.b...  1.3 us

profile of v4, /device:TPU:1, one launch (start us, length us, event | category | flops | bytes accessed | tf_op | source)
XLA Modules:
  0.0 33.5 jit_solution(2908802679781514459)
XLA Ops:
  0.0 32.2 %shard_map.64 = (f32[4,640,256]{2,1,0:T(8,128)S(1)}, bf16[4,640,256]{2,1,0:T(8,128)(2,1)S(1)}, bf16[4,256,128]{2,1,0:T(8,128)(2,1)S(1)}) custom-call(bf16[512,640]{1,0:T(8,128)(2,1)} %q_hbm.1, bf16[64,2048]{1,0:T(8,128)(2,1)} %r_hbm.1, bf16[8,2048]{1,0:T(8,128)(2,1)} %p_hbm.1, s32[128]{0:T(128)} %g_hbm.1, s32[128]{0:T(128)} %l_hbm.1, s32[4,128]{1,0:T(4,128)} %bitcast.1), custom_call_target="tpu_custom_call" | custom-call | flops 536870912 | bytes 3145728 | tf_op jit(solution)/shard_map/pallas_call | solution.py:255
  32.2 1.3 %shard_map.65 = bf16[512,640]{1,0:T(8,128)(2,1)} custom-call(f32[4,640,256]{2,1,0:T(8,128)S(1)} %get-tuple-element.8.own, bf16[4,640,256]{2,1,0:T(8,128)(2,1)S(1)} %get-tuple-element.9.weights, bf16[4,256,128]{2,1,0:T(8,128)(2,1)S(1)} %get-tuple-element.10.rows), custom_call_target="tpu_custom_call" | custom-call | tf_op jit(solution)/shard_map/pallas_call | solution.py:282

commit v5 on v4

--- a/solution.py
+++ b/solution.py
@@ -139,8 +139,9 @@
             src = zz(-c * sign)
             if c == 6:
                 to_plane(src, 2 * sign, 0 if sign == 1 else 1, (kv,))
-            for o in (1, -1, 0):
-                to_plane(src, o, None, (kv,))
+        for o in (0, 1, -1):
+            for sign in (1, -1):
+                to_plane(zz(-c * sign), o * sign, None, (kv,))
 
     forward(0, 0, 3)
     forward(1, 0, 3)

time: 33.6 us -> 33.6 us (level)
  no operation moved by 1% of the time
where the time goes in v5:
time: 33.6 us; the launch traced here: 33.5 us
  Pallas kernels  33.5 us (100%)
    pallas_call x1, Pallas kernels, local(): pl.pallas_call(kernel, out_shape=(pltpu.VMEM((RESP_DEV, GROUP * RLEN, 2 *...  32.2 us
    pallas_call x1, Pallas kernels, local(): pl.pallas_call(weigh, out_shape=jax.ShapeDtypeStruct(queries.shape, jnp.b...  1.3 us

profile of v5, /device:TPU:1, one launch (start us, length us, event | category | flops | bytes accessed | tf_op | source)
XLA Modules:
  0.0 33.5 jit_solution(15696279010394769045)
XLA Ops:
  0.0 32.2 %shard_map.64 = (f32[4,640,256]{2,1,0:T(8,128)S(1)}, bf16[4,640,256]{2,1,0:T(8,128)(2,1)S(1)}, bf16[4,256,128]{2,1,0:T(8,128)(2,1)S(1)}) custom-call(bf16[512,640]{1,0:T(8,128)(2,1)} %q_hbm.1, bf16[64,2048]{1,0:T(8,128)(2,1)} %r_hbm.1, bf16[8,2048]{1,0:T(8,128)(2,1)} %p_hbm.1, s32[128]{0:T(128)} %g_hbm.1, s32[128]{0:T(128)} %l_hbm.1, s32[4,128]{1,0:T(4,128)} %bitcast.1), custom_call_target="tpu_custom_call" | custom-call | flops 536870912 | bytes 3145728 | tf_op jit(solution)/shard_map/pallas_call | solution.py:256
  32.2 1.3 %shard_map.65 = bf16[512,640]{1,0:T(8,128)(2,1)} custom-call(f32[4,640,256]{2,1,0:T(8,128)S(1)} %get-tuple-element.8.own, bf16[4,640,256]{2,1,0:T(8,128)(2,1)S(1)} %get-tuple-element.9.weights, bf16[4,256,128]{2,1,0:T(8,128)(2,1)S(1)} %get-tuple-element.10.rows), custom_call_target="tpu_custom_call" | custom-call | tf_op jit(solution)/shard_map/pallas_call | solution.py:283
